TPU v7x, 768 devices: a whole 4x8x12 slice. The times are simulated.
768 devices in a mesh: grp: 16 (over y, z_hi), sub: 48 (over x, z_lo, core).
Axes of the slice: x: 4, y: 8, z: 12 (z_hi: 2, z_lo: 6; z = z_hi * 6 + z_lo), core: 2. Of those that a mesh axis runs over, the one named last changes fastest.
Arguments:
- attn: bfloat16 [4096, 6144], P('grp', 'sub'), may hold values from -6 to 6
- grad_out: bfloat16 [4096, 12288], P('grp'), may hold values from -6 to 6
- w_values: bfloat16 [6144, 12288], P('sub', 'grp'), may hold values from -6 to 6
- w_scales: float32 [6144, 48], P('sub', 'grp'), may hold values from 0.00637888 to 0.02551552
Outputs:
- grad_attn: bfloat16 [4096, 6144], P('grp', 'sub')
- grad_w: bfloat16 [6144, 12288], P('sub', 'grp')
All inputs are finite; a program needn't handle non-finite values. Where the computation divides by a largest or mean magnitude, that divisor is 1e-20 or more.
Results may differ from a plain program's by a relative error of at most 0.0049.
Values may be sent and summed in bfloat16 or wider, within the bound.
A program may use at most 64 MiB of HBM per device.

v0:
```python
import jax
import jax.numpy as jnp
from jax import lax
from jax.sharding import PartitionSpec as P

BLOCK = 256


def on_device(attn, grad_out, w_values, w_scales):
    head_rows = w_values.shape[0]
    own_cols = w_values.shape[1]
    groups = lax.axis_size("grp")
    scale_full = jnp.repeat(w_scales, BLOCK, axis=1)
    w_local = (w_values.astype(jnp.float32) * scale_full).astype(jnp.bfloat16)
    input_sum = lax.dot_general(
        grad_out,
        lax.all_gather(w_local, "grp", axis=1, tiled=True),
        (((1,), (1,)), ((), ())),
        preferred_element_type=jnp.float32,
    )
    part = lax.dot_general(
        attn, grad_out, (((0,), (0,)), ((), ())), preferred_element_type=jnp.float32
    )
    full_cols = part.shape[1]
    blocks = part.reshape(head_rows, full_cols // BLOCK, BLOCK)
    largest = (jnp.max(jnp.abs(blocks), axis=2) + 1e-06).astype(jnp.bfloat16)
    quant = (blocks / largest.astype(jnp.float32)[:, :, None]).astype(jnp.bfloat16)
    quant = quant.reshape(head_rows, full_cols)
    got_quant, got_scale = (
        lax.all_to_all(quant, "grp", split_axis=1, concat_axis=0, tiled=True),
        lax.all_to_all(largest, "grp", split_axis=1, concat_axis=0, tiled=True),
    )
    restored = got_quant.astype(jnp.float32).reshape(groups * head_rows, own_cols // BLOCK, BLOCK)
    restored = restored * got_scale.astype(jnp.float32)[:, :, None]
    summed = jnp.sum(restored.reshape(groups, head_rows, own_cols), axis=0)
    grad_attn = input_sum.astype(jnp.bfloat16)
    total = lax.psum(jnp.sum(summed * summed), ("grp", "sub"))
    count = head_rows * lax.axis_size("sub") * own_cols * groups
    clip = jnp.minimum(1.0, 0.5 * jnp.sqrt(jnp.float32(count)) / jnp.sqrt(total))
    return (grad_attn, (summed * clip).astype(jnp.bfloat16))


def solution(mesh):
    placed = (P("grp", "sub"), P("grp", None), P("sub", "grp"), P("sub", "grp"))
    return jax.shard_map(
        on_device,
        mesh=mesh,
        in_specs=placed,
        out_specs=(P("grp", "sub"), P("sub", "grp")),
        check_vma=False,
    )
```

profile of v0, /device:TPU:6, one launch (start us, length us, event | category | flops | bytes accessed | tf_op | source)
XLA Modules:
  0.0 485.0 jit_solution(1162271386761270872)
XLA Ops:
  7.2 0.8 copy-done
  8.0 7.1 %fusion.3 = (f32[128,12288]{1,0:T(8,128)S(1)}, f32[128,12288]{1,0:T(8,128)}) fusion(bf16[256,128]{1,0:T(8,128)(2,1)S(1)} %copy-done, bf16[256,12288]{1,0:T(8,128)(2,1)} %param.5), kind=kOutput, calls=%fused_computation.11 | convolution fusion | flops 806879232 | bytes 18939904 | tf_op jit(solution)/shard_map/dot_general | solution.py:21
  15.1 4.6 copy.26
  19.7 3.7 reduce_max.9
  24.1 19.9 %all-to-all-start.1 = ((bf16[128,16,3]{0,2,1:T(4,128)(2,1)}), bf16[128,16,3]{0,2,1:T(4,128)(2,1)S(1)}, u32[]{:S(2)}, u32[]{:S(2)}) async-start(bf16[128,16,3]{0,2,1:T(4,128)(2,1)} %convert_element_type.67), calls=%async_computation.1 | async-start | bytes 32768 | tf_op jit(solution)/shard_map/all_to_all | solution.py:31
  44.1 0.9 div.14
  45.0 4.9 %copy.27 = f32[16,8,48,256]{3,1,2,0:T(8,128)S(1)} copy(f32[16,8,48,256]{3,2,1,0:T(8,128)S(1)} %bitcast.32) | data formatting | bytes 12582912
  49.9 0.9 divide_convert_fusion
  50.8 2.9 copy.25
  53.6 5.2 %all-to-all-done.1 = bf16[128,16,3]{0,2,1:T(4,128)(2,1)S(1)} async-done(((bf16[128,16,3]{0,2,1:T(4,128)(2,1)}), bf16[128,16,3]{0,2,1:T(4,128)(2,1)S(1)}, u32[]{:S(2)}, u32[]{:S(2)}) %all-to-all-start.1) | async-done | bytes 12320 | tf_op jit(solution)/shard_map/all_to_all | solution.py:31
  58.8 9.4 %all-to-all-start = ((bf16[128,16,768]{0,2,1:T(8,128)(2,1)}), bf16[128,16,768]{0,2,1:T(8,128)(2,1)S(1)}, u32[]{:S(2)}, u32[]{:S(2)}) async-start(bf16[128,16,768]{0,2,1:T(8,128)(2,1)} %bitcast.2), calls=%async_computation | async-start | bytes 6291456 | tf_op jit(solution)/shard_map/all_to_all | solution.py:30
  68.3 1.1 copy.18
  69.4 0.7 fusion.2
  70.2 0.8 mul.24
  70.9 4.1 copy.28
  75.0 283.5 %all-gather.2.cloned.1.call-done = bf16[128,12288]{0,1:T(8,128)(2,1)} async-done(((bf16[128,768]{0,1:T(8,128)(2,1)}), bf16[128,12288]{0,1:T(8,128)(2,1)}) %all-gather.2.cloned.1.call-update) | async-done | bytes 3145744 | tf_op jit(solution)/shard_map/all_gather | solution.py:17
  358.5 6.0 %fusion.1 = bf16[256,128]{0,1:T(8,128)(2,1)S(1)} fusion(bf16[128,12288]{0,1:T(8,128)(2,1)} %all-gather.2.cloned.1.call-done, bf16[256,12288]{1,0:T(8,128)(2,1)} %param.5), kind=kOutput, calls=%fused_computation.4 | convolution fusion | flops 805339136 | bytes 9502720 | tf_op jit(solution)/shard_map/dot_general | solution.py:15
  364.5 5.6 %fusion = f32[128,768]{0,1:T(8,128)S(1)} fusion(f32[96,8,16,128]{3,2,1,0:T(8,128)} %copy.28, bf16[128,16,768]{0,2,1:T(8,128)(2,1)S(1)} %all-to-all-done), kind=kLoop, calls=%fused_computation.1 | loop fusion | flops 4620288 | bytes 9830400 | tf_op jit(solution)/shard_map/reduce_sum | solution.py:35
  370.1 0.7 copy-done.1
  370.9 0.7 multiply_reduce_fusion
  371.6 0.7 copy.23
  372.3 103.3 %psum.7 = f32[]{:T(128)} all-reduce(f32[]{:T(128)} %multiply_reduce_fusion), channel_id=1, replica_groups=mesh['grp'=16,'sub'=48] {'grp','sub'}, use_global_device_ids=true, to_apply=%region_3.0 | all-reduce | flops 1 | bytes 8 | tf_op jit(solution)/shard_map/psum | solution.py:37
  476.3 1.0 multiply_convert_fusion
  477.3 0.8 copy.24
  (17 shorter events, 0.9 us)
Async XLA Ops:
  7.2 0.8 copy-start
  24.1 34.7 %all-to-all-start.1 = ((bf16[128,16,3]{0,2,1:T(4,128)(2,1)}), bf16[128,16,3]{0,2,1:T(4,128)(2,1)S(1)}, u32[]{:S(2)}, u32[]{:S(2)}) async-start(bf16[128,16,3]{0,2,1:T(4,128)(2,1)} %convert_element_type.67), calls=%async_computation.1 | async-start | bytes 32768 | tf_op jit(solution)/shard_map/all_to_all | solution.py:31
  44.1 5.8 %slice-start = ((s8[6291456]{0:T(1024)(128)(4,1)}), s8[4194304]{0:T(1024)(128)(4,1)S(1)}, s32[]{:S(2)}) async-start(s8[6291456]{0:T(1024)(128)(4,1)} %bitcast.36), calls=%async_computation.3 | async-start | bytes 8388608
  44.9 4.9 %slice-start.1 = ((s8[6291456]{0:T(1024)(128)(4,1)}), s8[2097152]{0:T(1024)(128)(4,1)S(1)}, s32[]{:S(2)}) async-start(s8[6291456]{0:T(1024)(128)(4,1)} %bitcast.36), calls=%async_computation.4 | async-start | bytes 4194304
  50.8 18.6 %copy-start.2 = (f32[128,3]{0,1:T(4,128)S(1)}, f32[128,3]{0,1:T(4,128)}, u32[]{:S(2)}) copy-start(f32[128,3]{0,1:T(4,128)} %param.7) | copy-start | bytes 4612
  58.8 305.7 %all-to-all-start = ((bf16[128,16,768]{0,2,1:T(8,128)(2,1)}), bf16[128,16,768]{0,2,1:T(8,128)(2,1)S(1)}, u32[]{:S(2)}, u32[]{:S(2)}) async-start(bf16[128,16,768]{0,2,1:T(8,128)(2,1)} %bitcast.2), calls=%async_computation | async-start | bytes 6291456 | tf_op jit(solution)/shard_map/all_to_all | solution.py:30
  68.3 290.3 %all-gather.2.cloned.1.call-start = ((), (), s32[]{:S(2)}) async-start(), calls=%async_computation.2 | async-start | bytes 3342336 | tf_op jit(solution)/shard_map/all_gather | solution.py:17
  370.1 0.8 copy-start.1
Sparse Core Ops, SparseCore 0:
  73.4 285.0 all-gather.1
where the time goes:
time: 488 us; the launch traced here: 485 us
  waiting for transfers between devices  289 us (59%)
  blocking collectives  103 us (21%)
  starting transfers between devices  29.4 us (6%)
  local copies, waits for them, and re-layouts  23.1 us (5%)
  between operations  14.9 us (3%)
  matrix products  13 us (3%)
  other arithmetic  12.6 us (3%)
    all_gather x1, waiting for transfers between devices, on_device(): lax.all_gather(w_local, 'grp', axis=1, tiled=True)  284 us
    psum x1, blocking collectives, on_device(): total = lax.psum(jnp.sum(summed * summed), ('grp', 'sub'))  103 us
    all_to_all x1, starting transfers between devices, on_device(): lax.all_to_all(largest, 'grp', split_axis=1, concat_axis=0, tiled=True)  19.9 us
    unnamed x16, local copies, waits for them, and re-layouts  17.9 us
  transfers between devices with their start and end apart: 3, of which 2 were waited for; matrix products, arithmetic and copies ran while one was open for 5% of the time, Pallas kernels for 0%

commit v1 on v0

v1 whole, which is shorter than its diff:
```python
import jax
import jax.numpy as jnp
from jax import lax
from jax.experimental import pallas as pl
from jax.experimental.pallas import tpu as pltpu
from jax.sharding import PartitionSpec as P

BLOCK = 256
NY, NZH, NX, NZL, NC = 8, 2, 4, 6, 2
NZ = NZH * NZL
MESH = pl.DeviceIdType.MESH
F32, BF16 = jnp.float32, jnp.bfloat16

UP = ((4, 0), (3, 1), (3, 0), (2, 1), (2, 0), (1, 1), (1, 0))
DOWN = ((4, 1), (3, 0), (3, 1), (2, 0), (2, 1), (1, 0), (1, 1))


def body(
    attn_ref, go_hbm, wv_ref, ws_ref, ga_ref, gw_ref,
    go, attn_t, w_own, w_got, rs_send, rs_got, own_sum, z_send, z_got, tile, tiles,
    go_sem, wz_sem, ag_sem, rs_sem, z_sem, ar_sem,
):
    grp, sub = lax.axis_index("grp"), lax.axis_index("sub")
    y, zh = grp // NZH, grp % NZH
    x, zl, core = sub // (NZL * NC), (sub // NC) % NZL, sub % NC
    z, xc = zh * NZL + zl, x * NC + core
    cols = wv_ref.shape[1]

    def along_y(d):
        return (((y + d) % NY) * NZH + zh, sub)

    def along_z(d):
        other = (z + d) % NZ
        return (y * NZH + other // NZL, (x * NZL + other % NZL) * NC + core)

    def along_xc(d):
        other = (xc + d) % (NX * NC)
        return (grp, ((other // NC) * NZL + zl) * NC + other % NC)

    sent = []

    def send(src, dst, sems, to):
        copy = pltpu.make_async_remote_copy(
            src_ref=src, dst_ref=dst, send_sem=sems[0], recv_sem=sems[1],
            device_id=to, device_id_type=MESH,
        )
        copy.start()
        sent.append(copy)
        return copy

    barrier = pltpu.get_barrier_semaphore()
    partners = [along_y(d) for d in range(1, NY)] + [along_z(d) for d in range(1, NZ)]
    partners += [along_xc(d) for d in range(1, NX * NC)]
    for to in partners:
        pl.semaphore_signal(barrier, inc=1, device_id=to, device_id_type=MESH)

    loads = {}
    for d in (4, 3, 5, 2, 6, 1, 7, 0):
        for h in (0, 1):
            chunk = ((y + d) % NY) * NZH + h
            loads[d, h] = pltpu.make_async_copy(
                go_hbm.at[:, pl.ds(pl.multiple_of(chunk * cols, cols), cols)],
                go.at[d, h],
                go_sem.at[d, h],
            )
            loads[d, h].start()

    scaled = [
        (wv_ref[:, j * BLOCK:(j + 1) * BLOCK].astype(F32) * ws_ref[:, j:j + 1]).astype(BF16)
        for j in range(cols // BLOCK)
    ]
    w_own[zh] = jnp.concatenate(scaled, axis=1)
    attn_t[...] = attn_ref[...].T

    pl.semaphore_wait(barrier, len(partners))
    opposite = along_z(NZL)
    w_z = send(w_own.at[zh], w_own.at[zh], (wz_sem.at[0], wz_sem.at[1]), opposite)

    def part(d, h):
        if (d, h) in loads:
            loads.pop((d, h)).wait()
        return jnp.dot(attn_t[...], go[d, h], preferred_element_type=F32)

    ways = ((0, 1, UP), (1, -1, DOWN))
    got = {}
    for i in range(7):
        for way, sign, items in ways:
            d, h = items[i]
            piece = part((sign * d) % NY, h)
            if (way, d + 1, h) in got:
                before = got[way, d + 1, h]
                before[0].wait_recv()
                piece = piece + rs_got[way, before[1]].astype(F32)
            rs_send[way, i] = piece.astype(BF16)
            copy = send(
                rs_send.at[way, i], rs_got.at[way, i],
                (rs_sem.at[0, way, i], rs_sem.at[1, way, i]), along_y(sign),
            )
            got[way, d, h] = (copy, i)

    def pass_on(src, way, sign, d, h):
        return send(
            src, w_got.at[way, d - 1, h],
            (ag_sem.at[0, way, d - 1, h], ag_sem.at[1, way, d - 1, h]), along_y(sign),
        )

    w_z.wait_recv()
    gathered = {}
    for h in (0, 1):
        for way, sign, _ in ways:
            gathered[way, 1, h] = pass_on(w_own.at[h], way, sign, 1, h)

    for h in (0, 1):
        own_sum[h] = part(0, h)
    for i in (5, 6):
        for way, _, items in ways:
            h = items[i][1]
            got[way, 1, h][0].wait_recv()
            own_sum[h] += rs_got[way, i].astype(F32)
    z_send[...] = own_sum[1 - zh].astype(BF16)
    to_opposite = send(z_send, z_got, (z_sem.at[0], z_sem.at[1]), opposite)

    def product(d, h, w):
        return lax.dot_general(go[d % NY, h], w, (((1,), (1,)), ((), ())), preferred_element_type=F32)

    total = product(0, 0, w_own[0]) + product(0, 1, w_own[1])

    def ring_step(d, total):
        arrived = []
        for h in (0, 1):
            for way, sign, _ in ways:
                if (way, d, h) not in gathered:
                    continue
                gathered[way, d, h].wait_recv()
                arrived.append((way, sign, h))
                if d < 3 or (d == 3 and h == way):
                    gathered[way, d + 1, h] = pass_on(w_got.at[way, d - 1, h], way, sign, d + 1, h)
        for way, sign, h in arrived:
            total = total + product(-sign * d, h, w_got[way, d - 1, h])
        return total

    def spread(stage, first, count, along):
        copies = []
        for d in range(1, count):
            slot = first + d - 1
            copies.append(
                send(tile.at[stage], tiles.at[slot], (ar_sem.at[0, slot], ar_sem.at[1, slot]), along(d))
            )
        return copies

    def collect(stage, first, copies):
        value = tile[stage]
        for d, copy in enumerate(copies):
            copy.wait_recv()
            value = value + tiles[first + d]
        return value

    total = ring_step(1, total)
    to_opposite.wait_recv()
    summed = own_sum[zh] + z_got[...].astype(F32)
    own_sum[zh] = summed
    squares = jnp.sum((summed * summed).reshape(-1, 8, cols), axis=0)
    tile[0] = sum(squares[:, j * 128:(j + 1) * 128] for j in range(cols // 128))
    copies = spread(0, 0, NY, along_y)
    total = ring_step(2, total)
    tile[1] = collect(0, 0, copies)
    copies = spread(1, NY - 1, NZ, along_z)
    total = ring_step(3, total)
    tile[2] = collect(1, NY - 1, copies)
    copies = spread(2, NY + NZ - 2, NX * NC, along_xc)
    total = ring_step(4, total)
    ga_ref[...] = total.astype(BF16)
    squares = jnp.sum(collect(2, NY + NZ - 2, copies), keepdims=True)
    count = NY * NZH * NX * NZL * NC * own_sum.shape[1] * cols
    clip = jnp.minimum(1.0, 0.5 * jnp.sqrt(jnp.full((1, 1), count, F32)) / jnp.sqrt(squares))
    gw_ref[...] = (own_sum[zh] * clip).astype(BF16)
    for copy in sent:
        copy.wait_send()


def on_device(attn, grad_out, w_values, w_scales):
    tokens, head = attn.shape
    rows, cols = w_values.shape
    vmem = pl.BlockSpec(memory_space=pltpu.VMEM)
    dma = pltpu.SemaphoreType.DMA
    n_tiles = NY + NZ + NX * NC - 3
    return pl.pallas_call(
        body,
        out_shape=(
            jax.ShapeDtypeStruct((tokens, head), BF16),
            jax.ShapeDtypeStruct((rows, cols), BF16),
        ),
        in_specs=[vmem, pl.BlockSpec(memory_space=pl.ANY), vmem, vmem],
        out_specs=(vmem, vmem),
        scratch_shapes=[
            pltpu.VMEM((NY, 2, tokens, cols), BF16),
            pltpu.VMEM((head, tokens), BF16),
            pltpu.VMEM((2, rows, cols), BF16),
            pltpu.VMEM((2, 4, 2, rows, cols), BF16),
            pltpu.VMEM((2, 7, rows, cols), BF16),
            pltpu.VMEM((2, 7, rows, cols), BF16),
            pltpu.VMEM((2, rows, cols), F32),
            pltpu.VMEM((rows, cols), BF16),
            pltpu.VMEM((rows, cols), BF16),
            pltpu.VMEM((3, 8, 128), F32),
            pltpu.VMEM((n_tiles, 8, 128), F32),
            dma((NY, 2)),
            dma((2,)),
            dma((2, 2, 4, 2)),
            dma((2, 2, 7)),
            dma((2,)),
            dma((2, n_tiles)),
        ],
        compiler_params=pltpu.CompilerParams(
            collective_id=0, has_side_effects=True, vmem_limit_bytes=48 * 2**20
        ),
        cost_estimate=pl.CostEstimate(
            flops=4 * tokens * head * 16 * cols, bytes_accessed=8 * 2**20, transcendentals=0
        ),
    )(attn, grad_out, w_values, w_scales)


def solution(mesh):
    placed = (P("grp", "sub"), P("grp", None), P("sub", "grp"), P("sub", "grp"))
    return jax.shard_map(
        on_device,
        mesh=mesh,
        in_specs=placed,
        out_specs=(P("grp", "sub"), P("sub", "grp")),
        check_vma=False,
    )
```

time: 488 us -> 88.5 us (0.18)
  the two profiles are of different devices: /device:TPU:6 before, /device:TPU:1 now
where the time goes in v1:
time: 88.5 us; the launch traced here: 88.3 us
  Pallas kernels  83.8 us (95%)
  local copies, waits for them, and re-layouts  3.86 us (4%)
    pallas_call x1, Pallas kernels, on_device(): pl.pallas_call(body, out_shape=(jax.ShapeDtypeStruct((tokens, head), BF16...  83.8 us
    unnamed x7, local copies, waits for them, and re-layouts  3.86 us

profile of v1, /device:TPU:1, one launch (start us, length us, event | category | flops | bytes accessed | tf_op | source)
XLA Modules:
  0.0 88.3 jit_solution(15052038697863530823)
XLA Ops:
  0.6 0.8 copy.6.ws_ref
  1.4 0.0 copy-start
  1.4 0.9 %copy-done = bf16[128,768]{1,0:T(8,128)(2,1)S(1)} copy-done((bf16[128,768]{1,0:T(8,128)(2,1)S(1)}, bf16[128,768]{1,0:T(8,128)(2,1)}, u32[]{:S(2)}) %copy-start) | copy-done | bytes 196632
  2.3 0.0 copy-start.1
  2.3 0.8 copy-done.1
  3.2 83.8 %shard_map.59 = (bf16[256,128]{1,0:T(8,128)(2,1)S(1)}, bf16[128,768]{1,0:T(8,128)(2,1)S(1)}) custom-call(bf16[256,128]{1,0:T(8,128)(2,1)S(1)} %copy-done.1, bf16[256,12288]{1,0:T(8,128)(2,1)} %go_hbm.1, bf16[128,768]{1,0:T(8,128)(2,1)S(1)} %copy-done, f32[128,3]{1,0:T(8,128)S(1)} %copy.6.ws_ref), custom_call_target="tpu_custom_call" | custom-call | flops 1610612736 | bytes 8388608 | tf_op jit(solution)/shard_map/pallas_call | solution.py:187
  87.0 0.6 copy.9
  87.6 0.7 copy.10
Async XLA Ops:
  1.4 0.9 %copy-start = (bf16[128,768]{1,0:T(8,128)(2,1)S(1)}, bf16[128,768]{1,0:T(8,128)(2,1)}, u32[]{:S(2)}) copy-start(bf16[128,768]{1,0:T(8,128)(2,1)} %wv_ref.1) | copy-start | bytes 589828
  2.3 0.8 copy-start.1

commit v2 on v1

--- a/solution.py
+++ b/solution.py
@@ -11,20 +11,20 @@
 MESH = pl.DeviceIdType.MESH
 F32, BF16 = jnp.float32, jnp.bfloat16
 
-UP = ((4, 0), (3, 1), (3, 0), (2, 1), (2, 0), (1, 1), (1, 0))
-DOWN = ((4, 1), (3, 0), (3, 1), (2, 0), (2, 1), (1, 0), (1, 1))
+UP = ((4, 1), (3, 1), (2, 1), (1, 1), (3, 0), (2, 0), (1, 0))
+DOWN = ((3, 1), (2, 1), (1, 1), (4, 0), (3, 0), (2, 0), (1, 0))
 
 
 def body(
     attn_ref, go_hbm, wv_ref, ws_ref, ga_ref, gw_ref,
-    go, attn_t, w_own, w_got, rs_send, rs_got, own_sum, z_send, z_got, tile, tiles,
+    go, attn_t, w_own, w_got, rs_send, rs_got, own_part, own_sum, z_send, z_got, tile, tiles,
     go_sem, wz_sem, ag_sem, rs_sem, z_sem, ar_sem,
 ):
     grp, sub = lax.axis_index("grp"), lax.axis_index("sub")
     y, zh = grp // NZH, grp % NZH
     x, zl, core = sub // (NZL * NC), (sub // NC) % NZL, sub % NC
     z, xc = zh * NZL + zl, x * NC + core
-    cols = wv_ref.shape[1]
+    cols, half = wv_ref.shape[1], wv_ref.shape[0] // 2
 
     def along_y(d):
         return (((y + d) % NY) * NZH + zh, sub)
@@ -55,9 +55,9 @@
         pl.semaphore_signal(barrier, inc=1, device_id=to, device_id_type=MESH)
 
     loads = {}
-    for d in (4, 3, 5, 2, 6, 1, 7, 0):
-        for h in (0, 1):
-            chunk = ((y + d) % NY) * NZH + h
+    for h in (1, 0):
+        for d in (4, 3, 5, 2, 6, 1, 7, 0):
+            chunk = ((y + d) % NY) * NZH + (zh if h == 0 else 1 - zh)
             loads[d, h] = pltpu.make_async_copy(
                 go_hbm.at[:, pl.ds(pl.multiple_of(chunk * cols, cols), cols)],
                 go.at[d, h],
@@ -69,12 +69,12 @@
         (wv_ref[:, j * BLOCK:(j + 1) * BLOCK].astype(F32) * ws_ref[:, j:j + 1]).astype(BF16)
         for j in range(cols // BLOCK)
     ]
-    w_own[zh] = jnp.concatenate(scaled, axis=1)
+    w_own[0] = jnp.concatenate(scaled, axis=1)
     attn_t[...] = attn_ref[...].T
 
     pl.semaphore_wait(barrier, len(partners))
     opposite = along_z(NZL)
-    w_z = send(w_own.at[zh], w_own.at[zh], (wz_sem.at[0], wz_sem.at[1]), opposite)
+    w_z = send(w_own.at[0], w_own.at[1], (wz_sem.at[0], wz_sem.at[1]), opposite)
 
     def part(d, h):
         if (d, h) in loads:
@@ -83,20 +83,42 @@
 
     ways = ((0, 1, UP), (1, -1, DOWN))
     got = {}
-    for i in range(7):
+
+    def reduce_step(i):
         for way, sign, items in ways:
             d, h = items[i]
-            piece = part((sign * d) % NY, h)
-            if (way, d + 1, h) in got:
-                before = got[way, d + 1, h]
-                before[0].wait_recv()
-                piece = piece + rs_got[way, before[1]].astype(F32)
-            rs_send[way, i] = piece.astype(BF16)
-            copy = send(
-                rs_send.at[way, i], rs_got.at[way, i],
-                (rs_sem.at[0, way, i], rs_sem.at[1, way, i]), along_y(sign),
-            )
-            got[way, d, h] = (copy, i)
+            own_part[way] = part((sign * d) % NY, h)
+        for r in (0, 1):
+            for way, sign, items in ways:
+                d, h = items[i]
+                piece = own_part[way, pl.ds(r * half, half)]
+                if (way, d + 1, h, r) in got:
+                    before, place = got[way, d + 1, h, r]
+                    before.wait_recv()
+                    piece = piece + rs_got[way, place].astype(F32)
+                k = 2 * i + r
+                rs_send[way, k] = piece.astype(BF16)
+                copy = send(
+                    rs_send.at[way, k], rs_got.at[way, k],
+                    (rs_sem.at[0, way, k], rs_sem.at[1, way, k]), along_y(sign),
+                )
+                got[way, d, h, r] = (copy, k)
+
+    def reduce_end(h):
+        own_sum[h] = part(0, h)
+        for r in (0, 1):
+            for way, _, _ in ways:
+                copy, k = got[way, 1, h, r]
+                copy.wait_recv()
+                own_sum[h, pl.ds(r * half, half)] += rs_got[way, k].astype(F32)
+
+    for i in range(5):
+        reduce_step(i)
+    reduce_end(1)
+    z_send[...] = own_sum[1].astype(BF16)
+    to_opposite = send(z_send, z_got, (z_sem.at[0], z_sem.at[1]), opposite)
+    for i in (5, 6):
+        reduce_step(i)
 
     def pass_on(src, way, sign, d, h):
         return send(
@@ -110,32 +132,23 @@
         for way, sign, _ in ways:
             gathered[way, 1, h] = pass_on(w_own.at[h], way, sign, 1, h)
 
-    for h in (0, 1):
-        own_sum[h] = part(0, h)
-    for i in (5, 6):
-        for way, _, items in ways:
-            h = items[i][1]
-            got[way, 1, h][0].wait_recv()
-            own_sum[h] += rs_got[way, i].astype(F32)
-    z_send[...] = own_sum[1 - zh].astype(BF16)
-    to_opposite = send(z_send, z_got, (z_sem.at[0], z_sem.at[1]), opposite)
+    reduce_end(0)
 
     def product(d, h, w):
         return lax.dot_general(go[d % NY, h], w, (((1,), (1,)), ((), ())), preferred_element_type=F32)
 
     total = product(0, 0, w_own[0]) + product(0, 1, w_own[1])
 
-    def ring_step(d, total):
+    def ring_step(d, h, total):
         arrived = []
-        for h in (0, 1):
-            for way, sign, _ in ways:
-                if (way, d, h) not in gathered:
-                    continue
-                gathered[way, d, h].wait_recv()
-                arrived.append((way, sign, h))
-                if d < 3 or (d == 3 and h == way):
-                    gathered[way, d + 1, h] = pass_on(w_got.at[way, d - 1, h], way, sign, d + 1, h)
-        for way, sign, h in arrived:
+        for way, sign, _ in ways:
+            if (way, d, h) not in gathered:
+                continue
+            gathered[way, d, h].wait_recv()
+            arrived.append((way, sign))
+            if d < 3 or (d == 3 and h == way):
+                gathered[way, d + 1, h] = pass_on(w_got.at[way, d - 1, h], way, sign, d + 1, h)
+        for way, sign in arrived:
             total = total + product(-sign * d, h, w_got[way, d - 1, h])
         return total
 
@@ -155,25 +168,29 @@
             value = value + tiles[first + d]
         return value
 
-    total = ring_step(1, total)
+    total = ring_step(1, 0, total)
     to_opposite.wait_recv()
-    summed = own_sum[zh] + z_got[...].astype(F32)
-    own_sum[zh] = summed
+    summed = own_sum[0] + z_got[...].astype(F32)
+    own_sum[0] = summed
     squares = jnp.sum((summed * summed).reshape(-1, 8, cols), axis=0)
     tile[0] = sum(squares[:, j * 128:(j + 1) * 128] for j in range(cols // 128))
-    copies = spread(0, 0, NY, along_y)
-    total = ring_step(2, total)
+    copies = spread(0, 0, NX * NC, along_xc)
+    total = ring_step(1, 1, total)
     tile[1] = collect(0, 0, copies)
-    copies = spread(1, NY - 1, NZ, along_z)
-    total = ring_step(3, total)
-    tile[2] = collect(1, NY - 1, copies)
-    copies = spread(2, NY + NZ - 2, NX * NC, along_xc)
-    total = ring_step(4, total)
-    ga_ref[...] = total.astype(BF16)
-    squares = jnp.sum(collect(2, NY + NZ - 2, copies), keepdims=True)
+    copies = spread(1, NX * NC - 1, NZ, along_z)
+    total = ring_step(2, 0, total)
+    total = ring_step(2, 1, total)
+    tile[2] = collect(1, NX * NC - 1, copies)
+    copies = spread(2, NX * NC + NZ - 2, NY, along_y)
+    total = ring_step(3, 0, total)
+    total = ring_step(3, 1, total)
+    squares = jnp.sum(collect(2, NX * NC + NZ - 2, copies), keepdims=True)
     count = NY * NZH * NX * NZL * NC * own_sum.shape[1] * cols
     clip = jnp.minimum(1.0, 0.5 * jnp.sqrt(jnp.full((1, 1), count, F32)) / jnp.sqrt(squares))
-    gw_ref[...] = (own_sum[zh] * clip).astype(BF16)
+    gw_ref[...] = (own_sum[0] * clip).astype(BF16)
+    total = ring_step(4, 0, total)
+    total = ring_step(4, 1, total)
+    ga_ref[...] = total.astype(BF16)
     for copy in sent:
         copy.wait_send()
 
@@ -197,8 +214,9 @@
             pltpu.VMEM((head, tokens), BF16),
             pltpu.VMEM((2, rows, cols), BF16),
             pltpu.VMEM((2, 4, 2, rows, cols), BF16),
-            pltpu.VMEM((2, 7, rows, cols), BF16),
-            pltpu.VMEM((2, 7, rows, cols), BF16),
+            pltpu.VMEM((2, 14, rows // 2, cols), BF16),
+            pltpu.VMEM((2, 14, rows // 2, cols), BF16),
+            pltpu.VMEM((2, rows, cols), F32),
             pltpu.VMEM((2, rows, cols), F32),
             pltpu.VMEM((rows, cols), BF16),
             pltpu.VMEM((rows, cols), BF16),
@@ -207,7 +225,7 @@
             dma((NY, 2)),
             dma((2,)),
             dma((2, 2, 4, 2)),
-            dma((2, 2, 7)),
+            dma((2, 2, 14)),
             dma((2,)),
             dma((2, n_tiles)),
         ],

time: 88.5 us -> 87.7 us (level)
  the two profiles are of different devices: /device:TPU:1 before, /device:TPU:6 now
where the time goes in v2:
time: 87.7 us; the launch traced here: 87.4 us
  Pallas kernels  82.9 us (95%)
  local copies, waits for them, and re-layouts  3.86 us (4%)
    pallas_call x1, Pallas kernels, on_device(): pl.pallas_call(body, out_shape=(jax.ShapeDtypeStruct((tokens, head), BF16...  82.9 us
    unnamed x7, local copies, waits for them, and re-layouts  3.86 us

profile of v2, /device:TPU:6, one launch (start us, length us, event | category | flops | bytes accessed | tf_op | source)
XLA Modules:
  0.0 87.4 jit_solution(1050169511951805953)
XLA Ops:
  0.6 0.8 copy.6.ws_ref
  1.4 0.0 copy-start
  1.4 0.9 %copy-done = bf16[128,768]{1,0:T(8,128)(2,1)S(1)} copy-done((bf16[128,768]{1,0:T(8,128)(2,1)S(1)}, bf16[128,768]{1,0:T(8,128)(2,1)}, u32[]{:S(2)}) %copy-start) | copy-done | bytes 196632
  2.3 0.0 copy-start.1
  2.3 0.8 copy-done.1
  3.2 82.9 %shard_map.59 = (bf16[256,128]{1,0:T(8,128)(2,1)S(1)}, bf16[128,768]{1,0:T(8,128)(2,1)S(1)}) custom-call(bf16[256,128]{1,0:T(8,128)(2,1)S(1)} %copy-done.1, bf16[256,12288]{1,0:T(8,128)(2,1)} %go_hbm.1, bf16[128,768]{1,0:T(8,128)(2,1)S(1)} %copy-done, f32[128,3]{1,0:T(8,128)S(1)} %copy.6.ws_ref), custom_call_target="tpu_custom_call" | custom-call | flops 1610612736 | bytes 8388608 | tf_op jit(solution)/shard_map/pallas_call | solution.py:204
  86.1 0.6 copy.9
  86.8 0.7 copy.10
Async XLA Ops:
  1.4 0.9 %copy-start = (bf16[128,768]{1,0:T(8,128)(2,1)S(1)}, bf16[128,768]{1,0:T(8,128)(2,1)}, u32[]{:S(2)}) copy-start(bf16[128,768]{1,0:T(8,128)(2,1)} %wv_ref.1) | copy-start | bytes 589828
  2.3 0.8 copy-start.1

commit v3 on v2

--- a/solution.py
+++ b/solution.py
@@ -16,9 +16,9 @@
 
 
 def body(
-    attn_ref, go_hbm, wv_ref, ws_ref, ga_ref, gw_ref,
-    go, attn_t, w_own, w_got, rs_send, rs_got, own_part, own_sum, z_send, z_got, tile, tiles,
-    go_sem, wz_sem, ag_sem, rs_sem, z_sem, ar_sem,
+    attn_hbm, go_hbm, wv_hbm, ws_hbm, ga_ref, gw_ref,
+    attn_ref, wv_ref, ws_ref, go, attn_t, w_own, w_got, rs_send, rs_got, own_part, own_sum, z_send, z_got, tile, tiles,
+    in_sem, go_sem, wz_sem, ag_sem, rs_sem, z_sem, ar_sem,
 ):
     grp, sub = lax.axis_index("grp"), lax.axis_index("sub")
     y, zh = grp // NZH, grp % NZH
@@ -48,15 +48,15 @@
         sent.append(copy)
         return copy
 
-    barrier = pltpu.get_barrier_semaphore()
-    partners = [along_y(d) for d in range(1, NY)] + [along_z(d) for d in range(1, NZ)]
-    partners += [along_xc(d) for d in range(1, NX * NC)]
-    for to in partners:
-        pl.semaphore_signal(barrier, inc=1, device_id=to, device_id_type=MESH)
-
+    inputs = [
+        pltpu.make_async_copy(src, dst, in_sem.at[i])
+        for i, (src, dst) in enumerate(((attn_hbm, attn_ref), (wv_hbm, wv_ref), (ws_hbm, ws_ref)))
+    ]
+    for copy in inputs:
+        copy.start()
     loads = {}
     for h in (1, 0):
-        for d in (4, 3, 5, 2, 6, 1, 7, 0):
+        for d in (4, 5, 3, 6, 2, 7, 1, 0):
             chunk = ((y + d) % NY) * NZH + (zh if h == 0 else 1 - zh)
             loads[d, h] = pltpu.make_async_copy(
                 go_hbm.at[:, pl.ds(pl.multiple_of(chunk * cols, cols), cols)],
@@ -65,16 +65,16 @@
             )
             loads[d, h].start()
 
-    scaled = [
-        (wv_ref[:, j * BLOCK:(j + 1) * BLOCK].astype(F32) * ws_ref[:, j:j + 1]).astype(BF16)
-        for j in range(cols // BLOCK)
-    ]
-    w_own[0] = jnp.concatenate(scaled, axis=1)
+    barrier = pltpu.get_barrier_semaphore()
+    partners = [along_y(d) for d in (1, 7, 2, 6, 3, 5, 4)] + [along_z(d) for d in range(1, NZ)]
+    partners += [along_xc(d) for d in range(1, NX * NC)]
+    for to in partners:
+        pl.semaphore_signal(barrier, inc=1, device_id=to, device_id_type=MESH)
+
+    inputs[0].wait()
     attn_t[...] = attn_ref[...].T
-
     pl.semaphore_wait(barrier, len(partners))
     opposite = along_z(NZL)
-    w_z = send(w_own.at[0], w_own.at[1], (wz_sem.at[0], wz_sem.at[1]), opposite)
 
     def part(d, h):
         if (d, h) in loads:
@@ -112,26 +112,38 @@
                 copy.wait_recv()
                 own_sum[h, pl.ds(r * half, half)] += rs_got[way, k].astype(F32)
 
-    for i in range(5):
+    def pass_on(src, way, sign, d, h):
+        return send(
+            src, w_got.at[way, d - 1, h],
+            (ag_sem.at[0, way, d - 1, h], ag_sem.at[1, way, d - 1, h]), along_y(sign),
+        )
+
+    gathered = {}
+
+    def first_pass(h):
+        for way, sign, _ in ways:
+            gathered[way, 1, h] = pass_on(w_own.at[h], way, sign, 1, h)
+
+    reduce_step(0)
+    for copy in inputs[1:]:
+        copy.wait()
+    for j in range(cols // BLOCK):
+        scale = jnp.broadcast_to(ws_ref[j:j + 1, :], (ws_ref.shape[1], ws_ref.shape[1])).T
+        for k in range(j * BLOCK, (j + 1) * BLOCK, scale.shape[1]):
+            piece = slice(k, k + scale.shape[1])
+            w_own[0, :, piece] = (wv_ref[:, piece].astype(F32) * scale).astype(BF16)
+    w_z = send(w_own.at[0], w_own.at[1], (wz_sem.at[0], wz_sem.at[1]), opposite)
+    for i in (1, 2, 3, 4):
         reduce_step(i)
+    first_pass(0)
     reduce_end(1)
     z_send[...] = own_sum[1].astype(BF16)
     to_opposite = send(z_send, z_got, (z_sem.at[0], z_sem.at[1]), opposite)
     for i in (5, 6):
         reduce_step(i)
 
-    def pass_on(src, way, sign, d, h):
-        return send(
-            src, w_got.at[way, d - 1, h],
-            (ag_sem.at[0, way, d - 1, h], ag_sem.at[1, way, d - 1, h]), along_y(sign),
-        )
-
     w_z.wait_recv()
-    gathered = {}
-    for h in (0, 1):
-        for way, sign, _ in ways:
-            gathered[way, 1, h] = pass_on(w_own.at[h], way, sign, 1, h)
-
+    first_pass(1)
     reduce_end(0)
 
     def product(d, h, w):
@@ -207,9 +219,12 @@
             jax.ShapeDtypeStruct((tokens, head), BF16),
             jax.ShapeDtypeStruct((rows, cols), BF16),
         ),
-        in_specs=[vmem, pl.BlockSpec(memory_space=pl.ANY), vmem, vmem],
+        in_specs=[pl.BlockSpec(memory_space=pltpu.HBM)] * 4,
         out_specs=(vmem, vmem),
         scratch_shapes=[
+            pltpu.VMEM((tokens, head), BF16),
+            pltpu.VMEM((rows, cols), BF16),
+            pltpu.VMEM((cols // BLOCK, rows), F32),
             pltpu.VMEM((NY, 2, tokens, cols), BF16),
             pltpu.VMEM((head, tokens), BF16),
             pltpu.VMEM((2, rows, cols), BF16),
@@ -222,6 +237,7 @@
             pltpu.VMEM((rows, cols), BF16),
             pltpu.VMEM((3, 8, 128), F32),
             pltpu.VMEM((n_tiles, 8, 128), F32),
+            dma((3,)),
             dma((NY, 2)),
             dma((2,)),
             dma((2, 2, 4, 2)),
@@ -230,12 +246,12 @@
             dma((2, n_tiles)),
         ],
         compiler_params=pltpu.CompilerParams(
-            collective_id=0, has_side_effects=True, vmem_limit_bytes=48 * 2**20
+            collective_id=0, has_side_effects=True, vmem_limit_bytes=40 * 2**20
         ),
         cost_estimate=pl.CostEstimate(
             flops=4 * tokens * head * 16 * cols, bytes_accessed=8 * 2**20, transcendentals=0
         ),
-    )(attn, grad_out, w_values, w_scales)
+    )(*(pltpu.with_memory_space_constraint(a, pltpu.HBM) for a in (attn, grad_out, w_values, w_scales.T)))
 
 
 def solution(mesh):

time: 87.7 us -> 84.9 us (0.968)
  local copies, waits for them, and re-layouts: 3.86 us -> 1.31 us
    unnamed x7 -> x2, local copies, waits for them, and re-layouts: 3.86 us -> 1.31 us
where the time goes in v3:
time: 84.9 us; the launch traced here: 84.7 us
  Pallas kernels  82.8 us (98%)
  local copies, waits for them, and re-layouts  1.31 us (2%)
    pallas_call x1, Pallas kernels, on_device(): pl.pallas_call(body, out_shape=(jax.ShapeDtypeStruct((tokens, head), BF16...  82.8 us

profile of v3, /device:TPU:6, one launch (start us, length us, event | category | flops | bytes accessed | tf_op | source)
XLA Modules:
  0.0 84.7 jit_solution(1973501799850675681)
XLA Ops:
  0.6 82.8 %shard_map.59 = (bf16[256,128]{1,0:T(8,128)(2,1)S(1)}, bf16[128,768]{1,0:T(8,128)(2,1)S(1)}) custom-call(bf16[256,128]{1,0:T(8,128)(2,1)} %attn_hbm.1, bf16[256,12288]{1,0:T(8,128)(2,1)} %go_hbm.1, bf16[128,768]{1,0:T(8,128)(2,1)} %wv_hbm.1, f32[3,128]{1,0:T(4,128)} %bitcast.1), custom_call_target="tpu_custom_call" | custom-call | flops 1610612736 | bytes 8388608 | tf_op jit(solution)/shard_map/pallas_call | solution.py:216
  83.4 0.6 copy.8
  84.0 0.7 copy.9

commit v4 on v3

--- a/solution.py
+++ b/solution.py
@@ -24,7 +24,7 @@
     y, zh = grp // NZH, grp % NZH
     x, zl, core = sub // (NZL * NC), (sub // NC) % NZL, sub % NC
     z, xc = zh * NZL + zl, x * NC + core
-    cols, half = wv_ref.shape[1], wv_ref.shape[0] // 2
+    cols, half, small = wv_ref.shape[1], wv_ref.shape[0] // 2, wv_ref.shape[0] // 4
 
     def along_y(d):
         return (((y + d) % NY) * NZH + zh, sub)
@@ -88,15 +88,15 @@
         for way, sign, items in ways:
             d, h = items[i]
             own_part[way] = part((sign * d) % NY, h)
-        for r in (0, 1):
+        for r in range(4):
             for way, sign, items in ways:
                 d, h = items[i]
-                piece = own_part[way, pl.ds(r * half, half)]
+                piece = own_part[way, pl.ds(r * small, small)]
                 if (way, d + 1, h, r) in got:
                     before, place = got[way, d + 1, h, r]
                     before.wait_recv()
                     piece = piece + rs_got[way, place].astype(F32)
-                k = 2 * i + r
+                k = 4 * i + r
                 rs_send[way, k] = piece.astype(BF16)
                 copy = send(
                     rs_send.at[way, k], rs_got.at[way, k],
@@ -106,23 +106,24 @@
 
     def reduce_end(h):
         own_sum[h] = part(0, h)
-        for r in (0, 1):
+        for r in range(4):
             for way, _, _ in ways:
                 copy, k = got[way, 1, h, r]
                 copy.wait_recv()
-                own_sum[h, pl.ds(r * half, half)] += rs_got[way, k].astype(F32)
-
-    def pass_on(src, way, sign, d, h):
+                own_sum[h, pl.ds(r * small, small)] += rs_got[way, k].astype(F32)
+
+    def pass_on(src, way, sign, d, h, q):
         return send(
-            src, w_got.at[way, d - 1, h],
-            (ag_sem.at[0, way, d - 1, h], ag_sem.at[1, way, d - 1, h]), along_y(sign),
+            src, w_got.at[way, d - 1, h, pl.ds(q * half, half)],
+            (ag_sem.at[0, way, d - 1, h, q], ag_sem.at[1, way, d - 1, h, q]), along_y(sign),
         )
 
     gathered = {}
 
     def first_pass(h):
         for way, sign, _ in ways:
-            gathered[way, 1, h] = pass_on(w_own.at[h], way, sign, 1, h)
+            for q in (0, 1):
+                gathered[way, 1, h, q] = pass_on(w_own.at[h, pl.ds(q * half, half)], way, sign, 1, h, q)
 
     reduce_step(0)
     for copy in inputs[1:]:
@@ -153,13 +154,16 @@
 
     def ring_step(d, h, total):
         arrived = []
-        for way, sign, _ in ways:
-            if (way, d, h) not in gathered:
-                continue
-            gathered[way, d, h].wait_recv()
-            arrived.append((way, sign))
-            if d < 3 or (d == 3 and h == way):
-                gathered[way, d + 1, h] = pass_on(w_got.at[way, d - 1, h], way, sign, d + 1, h)
+        for q in (0, 1):
+            for way, sign, _ in ways:
+                if (way, d, h, q) not in gathered:
+                    continue
+                gathered[way, d, h, q].wait_recv()
+                if q:
+                    arrived.append((way, sign))
+                if d < 3 or (d == 3 and h == way):
+                    src = w_got.at[way, d - 1, h, pl.ds(q * half, half)]
+                    gathered[way, d + 1, h, q] = pass_on(src, way, sign, d + 1, h, q)
         for way, sign in arrived:
             total = total + product(-sign * d, h, w_got[way, d - 1, h])
         return total
@@ -229,8 +233,8 @@
             pltpu.VMEM((head, tokens), BF16),
             pltpu.VMEM((2, rows, cols), BF16),
             pltpu.VMEM((2, 4, 2, rows, cols), BF16),
-            pltpu.VMEM((2, 14, rows // 2, cols), BF16),
-            pltpu.VMEM((2, 14, rows // 2, cols), BF16),
+            pltpu.VMEM((2, 28, rows // 4, cols), BF16),
+            pltpu.VMEM((2, 28, rows // 4, cols), BF16),
             pltpu.VMEM((2, rows, cols), F32),
             pltpu.VMEM((2, rows, cols), F32),
             pltpu.VMEM((rows, cols), BF16),
@@ -240,8 +244,8 @@
             dma((3,)),
             dma((NY, 2)),
             dma((2,)),
-            dma((2, 2, 4, 2)),
-            dma((2, 2, 14)),
+            dma((2, 2, 4, 2, 2)),
+            dma((2, 2, 28)),
             dma((2,)),
             dma((2, n_tiles)),
         ],

time: 84.9 us -> 83.9 us (0.988)
  Pallas kernels: 82.8 us -> 81.8 us
    pallas_call x1, Pallas kernels: 82.8 us -> 81.8 us  [on_device(): pl.pallas_call(body, out_shape=(jax.ShapeDtypeStruct((tokens, head), BF16...]
where the time goes in v4:
time: 83.9 us; the launch traced here: 83.7 us
  Pallas kernels  81.8 us (97%)
  local copies, waits for them, and re-layouts  1.31 us (2%)
    pallas_call x1, Pallas kernels, on_device(): pl.pallas_call(body, out_shape=(jax.ShapeDtypeStruct((tokens, head), BF16...  81.8 us

profile of v4, /device:TPU:6, one launch (start us, length us, event | category | flops | bytes accessed | tf_op | source)
XLA Modules:
  0.0 83.7 jit_solution(9204227568362543614)
XLA Ops:
  0.6 81.8 %shard_map.59 = (bf16[256,128]{1,0:T(8,128)(2,1)S(1)}, bf16[128,768]{1,0:T(8,128)(2,1)S(1)}) custom-call(bf16[256,128]{1,0:T(8,128)(2,1)} %attn_hbm.1, bf16[256,12288]{1,0:T(8,128)(2,1)} %go_hbm.1, bf16[128,768]{1,0:T(8,128)(2,1)} %wv_hbm.1, f32[3,128]{1,0:T(4,128)} %bitcast.1), custom_call_target="tpu_custom_call" | custom-call | flops 1610612736 | bytes 8388608 | tf_op jit(solution)/shard_map/pallas_call | solution.py:220
  82.4 0.6 copy.8
  83.1 0.7 copy.9

commit v5 on v4

--- a/solution.py
+++ b/solution.py
@@ -66,7 +66,7 @@
             loads[d, h].start()
 
     barrier = pltpu.get_barrier_semaphore()
-    partners = [along_y(d) for d in (1, 7, 2, 6, 3, 5, 4)] + [along_z(d) for d in range(1, NZ)]
+    partners = [along_y(d) for d in (1, 7)] + [along_z(d) for d in range(1, NZ)]
     partners += [along_xc(d) for d in range(1, NX * NC)]
     for to in partners:
         pl.semaphore_signal(barrier, inc=1, device_id=to, device_id_type=MESH)

time: 83.9 us -> 83.8 us (level)
  no operation moved by 1% of the time
where the time goes in v5:
time: 83.8 us; the launch traced here: 83.7 us
  Pallas kernels  81.7 us (97%)
  local copies, waits for them, and re-layouts  1.31 us (2%)
    pallas_call x1, Pallas kernels, on_device(): pl.pallas_call(body, out_shape=(jax.ShapeDtypeStruct((tokens, head), BF16...  81.7 us

profile of v5, /device:TPU:6, one launch (start us, length us, event | category | flops | bytes accessed | tf_op | source)
XLA Modules:
  0.0 83.7 jit_solution(3490468676937343332)
XLA Ops:
  0.6 81.7 %shard_map.59 = (bf16[256,128]{1,0:T(8,128)(2,1)S(1)}, bf16[128,768]{1,0:T(8,128)(2,1)S(1)}) custom-call(bf16[256,128]{1,0:T(8,128)(2,1)} %attn_hbm.1, bf16[256,12288]{1,0:T(8,128)(2,1)} %go_hbm.1, bf16[128,768]{1,0:T(8,128)(2,1)} %wv_hbm.1, f32[3,128]{1,0:T(4,128)} %bitcast.1), custom_call_target="tpu_custom_call" | custom-call | flops 1610612736 | bytes 8388608 | tf_op jit(solution)/shard_map/pallas_call | solution.py:220
  82.4 0.6 copy.8
  83.0 0.7 copy.9
